TPU v7x, 256 devices: a whole 4x4x8 slice. The times are simulated.
256 devices in a mesh: ch: 4 (over y_lo, core), sp: 64 (over y_hi, z, x).
Axes of the slice: x: 4, y: 4 (y_hi: 2, y_lo: 2; y = y_hi * 2 + y_lo), z: 8, core: 2. Of those that a mesh axis runs over, the one named last changes fastest.
Arguments:
- latents: bfloat16 [256, 64, 90, 128], P('ch', 'sp'), may hold values from -6 to 6
- space_weight: bfloat16 [256, 9, 256], P('ch'), may hold values from -0.125 to 0.125
- space_bias: float32 [256], P('ch'), may hold values from -3 to 3
- time_weight: bfloat16 [3, 256, 256], P(None, 'ch'), may hold values from -0.21875 to 0.21875
- time_bias: float32 [256], P('ch'), may hold values from -3 to 3
Outputs:
- decoded: bfloat16 [256, 64, 90, 128], P('ch', 'sp')
All inputs are finite; a program needn't handle non-finite values.
Results may differ from a plain program's by a relative error of at most 0.0046.
Values may be sent and summed in bfloat16 or wider, within the bound.
A program may use at most 128 MiB of HBM per device.

v0:
```python
import jax
import jax.numpy as jnp
from jax import lax
from jax.sharding import PartitionSpec as P


def space_taps(carry, padded, weight_part, rows, cols):
    for tap in range(9):
        row_off, col_off = divmod(tap, 3)
        window = padded[:, :, row_off : row_off + rows, col_off : col_off + cols]
        carry = carry + jnp.einsum(
            "oi,ifhw->ofhw", weight_part[:, tap, :], window, preferred_element_type=jnp.float32
        )
    return carry


def lag_sum(carry, piece, weight_part, out_frames):
    for lag in range(3):
        carry = carry + jnp.einsum(
            "oi,ifp->ofp",
            weight_part[lag],
            piece[:, 2 - lag : 2 - lag + out_frames],
            preferred_element_type=jnp.float32,
        )
    return carry


def temporal_section(hidden_flat, channel_sum, time_bias):
    slabs = lax.all_to_all(hidden_flat, "sp", split_axis=2, concat_axis=1, tiled=True)
    lead = jnp.zeros((slabs.shape[0], 2, slabs.shape[2]), jnp.bfloat16)
    extended = jnp.concatenate([lead, slabs], axis=1)
    total = channel_sum(extended, extended.shape[1] - 2)
    temporal_slab = (total + time_bias[:, None, None]).astype(jnp.bfloat16)
    temporal = lax.all_to_all(temporal_slab, "sp", split_axis=1, concat_axis=2, tiled=True)
    return temporal


def on_device(latents, space_weight, space_bias, time_weight, time_bias):
    shard_ch, frame_count, rows, cols = latents.shape
    start_carry = jnp.zeros((space_weight.shape[0], frame_count, rows, cols), jnp.float32)
    padded = jnp.pad(
        lax.all_gather(latents, "ch", axis=0, tiled=True), ((0, 0), (0, 0), (1, 1), (1, 1))
    )
    spatial = space_taps(start_carry, padded, space_weight, rows, cols)
    hidden = jax.nn.silu(spatial + space_bias[:, None, None, None]).astype(jnp.bfloat16)
    hidden_flat = hidden.reshape(hidden.shape[0], frame_count, rows * cols)

    def channel_sum(extended, out_frames):
        begin = jnp.zeros((time_weight.shape[1], out_frames, extended.shape[2]), jnp.float32)
        return lag_sum(
            begin, lax.all_gather(extended, "ch", axis=0, tiled=True), time_weight, out_frames
        )

    temporal = temporal_section(hidden_flat, channel_sum, time_bias)
    inputs_flat = latents.reshape(shard_ch, frame_count, rows * cols)
    decoded = (inputs_flat.astype(jnp.float32) + temporal.astype(jnp.float32)).astype(jnp.bfloat16)
    return decoded.reshape(latents.shape)


def solution(mesh):
    return jax.shard_map(
        on_device,
        mesh=mesh,
        in_specs=(
            P("ch", "sp", None, None),
            P("ch", None, None),
            P("ch"),
            P(None, "ch", None),
            P("ch"),
        ),
        out_specs=P("ch", "sp", None, None),
        check_vma=False,
    )
```

profile of v0, /device:TPU:1, one launch (start us, length us, event | category | flops | bytes accessed | tf_op | source)
XLA Modules:
  0.0 474.0 jit_solution(5669678473931049948)
XLA Ops:
  6.5 0.7 all-gather.3.cloned.1.call-update
  7.3 0.0 all-gather.5.cloned.1.call-start
  7.3 69.4 %all-gather.3.cloned.1.call-done = bf16[256,1,90,128]{3,0,2,1:T(8,128)(2,1)} async-done(((bf16[64,1,90,128]{3,0,2,1:T(8,128)(2,1)}), bf16[256,1,90,128]{3,0,2,1:T(8,128)(2,1)}) %all-gather.3.cloned.1.call-update) | async-done | bytes 5898256 | tf_op jit(solution)/shard_map/all_gather | solution.py:42
  76.7 4.7 fusion.1
  81.4 1.9 fusion.10
  83.3 1.9 fusion.13
  85.1 1.9 fusion.16
  87.0 1.1 fusion.19
  88.1 3.5 fusion.22
  91.6 2.8 fusion.4
  94.4 3.5 fusion.7
  97.9 6.2 %multiply_convert_fusion = bf16[64,90,128]{2,0,1:T(8,128)(2,1)} fusion(f32[90,128,64]{1,2,0:T(8,128)} %fusion.22, f32[90,128,64]{1,2,0:T(8,128)S(1)} %fusion.19, f32[90,128,64]{1,2,0:T(8,128)S(1)} %fusion.16, f32[90,128,64]{1,2,0:T(8,128)S(1)} %fusion.13, f32[90,128,64]{1,2,0:T(8,128)S(1)} %fusion.10, f32[90,128,64]{1,2,0:T(8,128)} %fusion.7, ...), kind=kOutput, calls=%fused_computation.35 | convolution fusion | flops 387809280 | bytes 30999040 | tf_op jit(solution)/shard_map/oi,ifhw->ofhw/dot_general | solution.py:11
  104.1 3.0 copy.30
  107.2 9.1 %reshape.110 = bf16[64,1,11520]{0,1,2:T(2,128)(2,1)} reshape(bf16[64,90,128]{0,2,1:T(8,128)(2,1)S(1)} %copy.30) | data formatting | bytes 2949120 | tf_op jit(solution)/shard_map/reshape | solution.py:46
  116.3 0.5 broadcast.14
  116.8 62.9 %reduce.2 = bf16[11520,64]{1,0:T(8,128)(2,1)S(1)} reduce(bf16[11520,1,64]{2,1,0:T(2,128)(2,1)} %bitcast.119, bf16[]{:T(256)} %broadcast.14), dimensions={1}, to_apply=%bitcast.113.reduce_sub_computation | reduce | bytes 2949122
  179.7 2.9 reshape.113
  182.6 51.0 %all_to_all.21 = bf16[64,2,5760]{2,1,0:T(2,128)(2,1)S(1)} all-to-all(bf16[64,2,5760]{2,1,0:T(2,128)(2,1)} %reshape.113), channel_id=1, replica_groups=mesh['ch'=4,'sp'=64] {'sp'}, dimensions={0} | all-to-all | bytes 2949120 | tf_op jit(solution)/shard_map/all_to_all | solution.py:29
  233.6 7.5 %reshape.114 = bf16[11520,1,64]{2,1,0:T(2,128)(2,1)} reshape(bf16[64,2,5760]{2,1,0:T(2,128)(2,1)S(1)} %all_to_all.21) | data formatting | bytes 2949120
  241.2 45.9 %bitcast_reduce_fusion = bf16[64,11520]{0,1:T(8,128)(2,1)} fusion(bf16[11520,1,64]{2,1,0:T(2,128)(2,1)} %reshape.114), kind=kLoop, calls=%fused_computation.71 | loop fusion | bytes 2949120 | tf_op jit(solution)/shard_map/all_to_all | solution.py:29
  287.1 3.9 reshape.111
  291.0 2.8 copy.35
  293.8 3.6 concatenate.3.clone
  297.4 82.1 %all-gather.5.cloned.1.call-done = bf16[256,66,180]{2,0,1:T(8,128)(2,1)} async-done(((bf16[64,66,180]{2,0,1:T(8,128)(2,1)}), bf16[256,66,180]{2,0,1:T(8,128)(2,1)}) %all-gather.5.cloned.1.call-update) | async-done | bytes 6082576 | tf_op jit(solution)/shard_map/all_gather | solution.py:51
  379.5 5.1 %fusion.32 = f32[64,180,64]{1,2,0:T(8,128)S(1)} fusion(bf16[256,66,180]{2,0,1:T(8,128)(2,1)} %all-gather.5.cloned.1.call-done, bf16[3,64,256]{2,1,0:T(8,128)(2,1)S(1)} %copy-done.3), kind=kOutput, calls=%fused_computation.38 | convolution fusion | flops 377487360 | bytes 9064448 | tf_op jit(solution)/shard_map/oi,ifp->ofp/dot_general | solution.py:19
  384.6 0.7 copy-done.1
  385.3 1.6 fusion.34
  386.9 2.1 fusion.30
  389.1 64.7 %all_to_all.22 = bf16[64,64,180]{2,0,1:T(8,128)(2,1)S(1)} all-to-all(bf16[64,64,180]{2,0,1:T(8,128)(2,1)S(1)} %fusion.30), channel_id=1, replica_groups=mesh['ch'=4,'sp'=64] {'sp'}, dimensions={1} | all-to-all | bytes 2949120 | tf_op jit(solution)/shard_map/all_to_all | solution.py:34
  453.8 3.2 copy.28
  457.0 5.6 %reshape.97 = f32[64,1,90,128]{3,2,0,1:T(8,128)S(1)} reshape(f32[64,64,180]{2,1,0:T(8,128)} %copy.28) | data formatting | bytes 5898240 | tf_op jit(solution)/shard_map/convert_element_type | solution.py:56
  462.6 4.4 fusion.27
  (13 shorter events, 0.0 us)
Async XLA Ops:
  6.5 70.1 %all-gather.3.cloned.1.call-start = ((), (), s32[]{:S(2)}) async-start(), calls=%async_computation.2 | async-start | bytes 7372800 | tf_op jit(solution)/shard_map/all_gather | solution.py:42
  7.3 74.1 %copy-start.2 = (bf16[64,9,256]{2,0,1:T(8,128)(2,1)S(1)}, bf16[64,9,256]{2,0,1:T(8,128)(2,1)}, u32[]{:S(2)}) copy-start(bf16[64,9,256]{2,0,1:T(8,128)(2,1)} %param.6) | copy-start | bytes 884740
  7.3 372.2 %all-gather.5.cloned.1.call-start = ((), (), s32[]{:S(2)}) async-start(), calls=%async_computation.3 | async-start | bytes 10813440 | tf_op jit(solution)/shard_map/all_gather | solution.py:51
  76.7 4.7 copy-start
  94.4 3.5 copy-start.4
  293.8 85.7 %copy-start.3 = (bf16[3,64,256]{2,1,0:T(8,128)(2,1)S(1)}, bf16[3,64,256]{2,1,0:T(8,128)(2,1)}, u32[]{:S(2)}) copy-start(bf16[3,64,256]{2,1,0:T(8,128)(2,1)} %param.8) | copy-start | bytes 294916
  379.5 5.8 %copy-start.1 = (bf16[256,66,180]{2,0,1:T(8,128)(2,1)S(1)}, bf16[256,66,180]{2,0,1:T(8,128)(2,1)}, u32[]{:S(2)}) copy-start(bf16[256,66,180]{2,0,1:T(8,128)(2,1)} %all-gather.5.cloned.1.call-done) | copy-start | bytes 18247684
  385.3 1.6 copy-start.5
Sparse Core Ops, SparseCore 0:
  9.2 67.4 all-gather.2
  297.5 81.9 all-gather.4
where the time goes:
time: 483 us; the launch traced here: 474 us
  waiting for transfers between devices  152 us (31%)
  blocking collectives  116 us (24%)
  local copies, waits for them, and re-layouts  88.8 us (18%)
  other arithmetic  67.3 us (14%)
  matrix products  36.3 us (8%)
  between operations  13.7 us (3%)
    all_gather x1, waiting for transfers between devices, channel_sum(): lax.all_gather(extended, 'ch', axis=0, tiled=True)  82.1 us
    all_gather x1, waiting for transfers between devices, on_device(): lax.all_gather(latents, 'ch', axis=0, tiled=True)  69.4 us
    all_to_all x1, blocking collectives, temporal_section(): lax.all_to_all(temporal_slab, 'sp', split_axis=1, concat_axis=2, tiled=True)  64.7 us
    unnamed x1, other arithmetic  62.9 us
    all_to_all x1, blocking collectives, temporal_section(): lax.all_to_all(hidden_flat, 'sp', split_axis=2, concat_axis=1, tiled=True)  51 us
    all_to_all x2, local copies, waits for them, and re-layouts, temporal_section(): lax.all_to_all(hidden_flat, 'sp', split_axis=2, concat_axis=1, tiled=True)  49.8 us
    dot_general x9, matrix products, space_taps(): jnp.einsum('oi,ifhw->ofhw', weight_part[:, tap, :], window, preferred_ele...  27.4 us
    unnamed x16, local copies, waits for them, and re-layouts  14.5 us
  transfers between devices with their start and end apart: 2, of which 2 were waited for; matrix products, arithmetic and copies ran while one was open for 0% of the time, Pallas kernels for 0%

commit v1 on v0

v1 whole, which is shorter than its diff:
```python
import functools

import jax
import jax.numpy as jnp
from jax import lax
from jax.experimental import pallas as pl
from jax.experimental.pallas import tpu as pltpu
from jax.sharding import PartitionSpec as P

MESH = pl.DeviceIdType.MESH
ROWS, COLS, CH, SHARD = 90, 128, 256, 64
PITCH = 96
NZ = 8
SPACE_K, TIME_K = 9 * CH, 3 * CH
ORDER = ((1, 2), (3, 0), (2, 3), (0, 2), (1, 0), (3, 2), (2, 0), (0, 3), (1, 3), (3, 1), (2, 2), (1, 1), (3, 3), (2, 1), (0, 1))


def chip_start(chip):
    return (45 * chip) // 4


def kernel(
    lat_hbm, weight_hbm, bias_hbm, out_ref,
    lat, flat, sent, taken, left, right, hidden, made, back, weight, bias, own_weight, own_bias,
    load_sem, in_send, in_recv, z_send, z_recv, swap_send, swap_recv, w_send, w_recv, out_send, out_recv,
):
    sp, q = lax.axis_index("sp"), lax.axis_index("ch")
    x = lax.rem(sp, 4)
    row_of_frames = sp // 4
    base = row_of_frames * 4
    z, yh = lax.rem(row_of_frames, NZ), row_of_frames // NZ
    hi, core = q // 2, lax.rem(q, 2)
    me = x * 4 + q
    has_prev = row_of_frames > 0
    has_next = row_of_frames < 2 * NZ - 1
    start = chip_start(2 * x + hi)
    short = lax.rem(2 * x + hi, 4) < 3

    def device(dx, fc):
        nx = lax.rem(x + dx, 4)
        nq = lax.rem(hi + fc // 2, 2) * 2 + lax.rem(core + fc % 2, 2)
        return nx, nq

    def ident(nx, nq):
        return {"sp": base + nx, "ch": nq}

    partner = {"sp": sp, "ch": hi * 2 + 1 - core}
    across = {"sp": (1 - yh) * 4 * NZ + z * 4 + x, "ch": (1 - hi) * 2 + core}

    loads = []
    for part in range(4):
        piece = pl.ds(part * 16, 16)
        copy = pltpu.make_async_copy(lat_hbm.at[piece, 0], lat.at[piece, pl.ds(0, ROWS)], load_sem.at[part])
        copy.start()
        loads.append(copy)
    load_weight = pltpu.make_async_copy(weight_hbm, own_weight, load_sem.at[4])
    load_bias = pltpu.make_async_copy(bias_hbm, own_bias, load_sem.at[5])
    load_weight.start()
    load_bias.start()
    barrier = pltpu.get_barrier_semaphore()
    for dx, fc in ORDER:
        pl.semaphore_signal(barrier, inc=1, device_id=ident(*device(dx, fc)), device_id_type=MESH)
    pl.semaphore_signal(barrier, inc=1, device_id=across, device_id_type=MESH)

    @pl.when(has_prev)
    def _():
        pl.semaphore_signal(barrier, inc=1, device_id={"sp": sp - 4, "ch": q}, device_id_type=MESH)

    sent[0] = jnp.zeros((SHARD, COLS), jnp.bfloat16)
    sent[ROWS + 1] = jnp.zeros((SHARD, COLS), jnp.bfloat16)
    for part in range(4):
        loads[part].wait()

        @pl.loop(part * 16, part * 16 + 16)
        def _(c):
            flat[pl.ds(pl.multiple_of(c * PITCH, PITCH), PITCH), :] = lat[c].astype(jnp.float32)

    @pl.loop(0, ROWS)
    def _(r):
        sent[r + 1] = flat[pl.ds(r, SHARD, stride=PITCH), :].astype(jnp.bfloat16)

    pl.semaphore_wait(barrier, 16 + has_next.astype(jnp.int32))

    load_weight.wait()
    load_bias.wait()
    weight_rows = pl.ds(pl.multiple_of(q * SHARD, SHARD), SHARD)
    weight_copies = []
    for i, there in enumerate((across, partner)):
        for j, (src, dst) in enumerate(((own_weight, weight), (own_bias, bias))):
            copy = pltpu.make_async_remote_copy(
                src_ref=src, dst_ref=dst.at[weight_rows], send_sem=w_send.at[2 * i + j], recv_sem=w_recv.at[2 * i + j],
                device_id=there, device_id_type=MESH,
            )
            copy.start()
            weight_copies.append(copy)
    keep_weight = pltpu.make_async_copy(own_weight, weight.at[weight_rows], load_sem.at[4])
    keep_bias = pltpu.make_async_copy(own_bias, bias.at[weight_rows], load_sem.at[5])
    keep_weight.start()
    keep_bias.start()

    def in_piece(chunk, t_chip, t_core):
        if chunk == 0:
            return chip_start(t_chip) + 10 * t_core, 4 * t_core, 4
        return chip_start(t_chip) + 4 + 3 * t_core, 4 - 3 * t_core, 3

    my_channels = pl.ds(pl.multiple_of(q * SHARD, SHARD), SHARD)
    in_copies = []
    for chunk in range(2):
        for k, (dx, fc) in enumerate(ORDER):
            nx, nq = device(dx, fc)
            src, dst, n = in_piece(chunk, 2 * nx + nq // 2, lax.rem(nq, 2))
            copy = pltpu.make_async_remote_copy(
                src_ref=sent.at[pl.ds(src, n)], dst_ref=taken.at[2 + x, pl.ds(dst, n), my_channels],
                send_sem=in_send.at[chunk, k], recv_sem=in_recv.at[chunk, me],
                device_id=ident(nx, nq), device_id_type=MESH,
            )
            copy.start()
            in_copies.append(copy)
        src, dst, n = in_piece(chunk, 2 * x + hi, core)
        pltpu.make_async_copy(
            sent.at[pl.ds(src, n)], taken.at[2 + x, pl.ds(dst, n), my_channels], in_recv.at[chunk, me]
        ).start()

    def z_copy(chunk, sx, sq):
        _, dst, n = in_piece(chunk, 0, core)
        return pltpu.make_async_remote_copy(
            src_ref=taken.at[2 + sx, pl.ds(dst, n), pl.ds(sq * SHARD, SHARD)],
            dst_ref=taken.at[sx - 2, pl.ds(dst, n), pl.ds(sq * SHARD, SHARD)],
            send_sem=z_send.at[chunk, (sx - 2) * 4 + sq], recv_sem=z_recv.at[chunk, (sx - 2) * 4 + sq],
            device_id={"sp": jnp.minimum(sp + 4, 8 * NZ - 1), "ch": q}, device_id_type=MESH,
        )

    def arrive(chunk):
        _, dst, n = in_piece(chunk, 0, core)
        for sx in (2, 3, 0, 1):
            for sq in range(4):
                got = taken.at[2 + sx, pl.ds(dst, n), pl.ds(sq * SHARD, SHARD)]
                pltpu.make_async_copy(got, got, in_recv.at[chunk, sx * 4 + sq]).wait()
                if sx >= 2:
                    pl.when(has_next)(lambda sx=sx, sq=sq: z_copy(chunk, sx, sq).start())

    def arrive_z(chunk):
        for sx in (2, 3):
            for sq in range(4):
                z_copy(chunk, sx, sq).wait_recv()

    def shift(slot, idx):
        row = taken[slot, idx].astype(jnp.float32)
        lane = lax.broadcasted_iota(jnp.int32, row.shape, 1)
        left[slot, idx] = jnp.where(lane == 0, 0.0, pltpu.roll(row, 1, 1)).astype(jnp.bfloat16)
        right[slot, idx] = jnp.where(lane == COLS - 1, 0.0, pltpu.roll(row, COLS - 1, 1)).astype(jnp.bfloat16)

    def conv(slot, pair):
        taps = []
        for dy in range(3):
            for buf in (left, taken, right):
                taps.append(jnp.concatenate([buf[slot, 2 * pair + dy], buf[slot, 2 * pair + dy + 1]], axis=1))
        rhs = jnp.concatenate(taps, axis=0)
        v = jnp.dot(weight[:, :SPACE_K], rhs, preferred_element_type=jnp.float32) + bias[:, 0:1]
        h = (v / (1.0 + jnp.exp(-v))).astype(jnp.bfloat16)
        hidden[slot, 2 * pair] = h[:, :COLS]
        hidden[slot, 2 * pair + 1] = h[:, COLS:]

    def temporal(frame, pair):
        lags = [
            jnp.concatenate([hidden[frame + 2 - lag, 2 * pair], hidden[frame + 2 - lag, 2 * pair + 1]], axis=1)
            for lag in range(3)
        ]
        rhs = jnp.concatenate(lags, axis=0)
        v = jnp.dot(weight[:, SPACE_K:], rhs, preferred_element_type=jnp.float32) + bias[:, 1:2]
        y = v.astype(jnp.bfloat16)
        made[frame, 2 * pair] = y[:, :COLS]
        made[frame, 2 * pair + 1] = y[:, COLS:]

    first_row = start + 6 * core

    def home_copy(frame, tq, pair, step, n):
        src = made.at[frame, pl.ds(2 * pair, n), pl.ds(pl.multiple_of(tq * SHARD, SHARD), SHARD)]
        dst = back.at[pl.ds(first_row + 2 * pair, n)]
        return src, dst, pltpu.make_async_remote_copy(
            src_ref=src, dst_ref=dst, send_sem=out_send.at[step, frame, tq], recv_sem=out_recv,
            device_id={"sp": base + frame, "ch": tq}, device_id_type=MESH,
        )

    def each_home(frame, pair, step, act_far, act_self):
        lacks = jnp.logical_and(jnp.logical_and(core == 1, short), pair == 2)
        for tq in range(4):
            is_me = jnp.logical_and(frame == x, tq == q)
            for n, fits in ((2, jnp.logical_not(lacks)), (1, lacks)):
                src, dst, far = home_copy(frame, tq, pair, step, n)
                pl.when(jnp.logical_and(fits, jnp.logical_not(is_me)))(functools.partial(act_far, far))
                pl.when(jnp.logical_and(fits, is_me))(functools.partial(act_self, src, dst))

    def go_home(frame, pair, step):
        each_home(
            frame, pair, step, lambda far: far.start(),
            lambda src, dst: pltpu.make_async_copy(src, dst, out_recv).start(),
        )

    def do_pair(pair, step):
        @pl.loop(2, 6)
        def _(slot):
            conv(slot, pair)

        @pl.loop(2, 4)
        def _(frame):
            temporal(frame, pair)
            go_home(frame, pair, step)

    def do_pair_z(pair, step):
        @pl.when(has_prev)
        def _():
            @pl.loop(0, 2)
            def _(slot):
                conv(slot, pair)

        @pl.when(jnp.logical_not(has_prev))
        def _():
            zero = jnp.zeros((CH, COLS), jnp.bfloat16)
            for slot in range(2):
                for k in range(2):
                    hidden[slot, 2 * pair + k] = zero

        @pl.loop(0, 2)
        def _(frame):
            temporal(frame, pair)
            go_home(frame, pair, step)

    def shift_rows(lo, hi_, idx0, n):
        @pl.loop(lo * n, hi_ * n)
        def _(i):
            shift(i // n, idx0 + lax.rem(i, n))

    arrive(0)
    for copy in weight_copies[:2]:
        copy.wait_recv()
    theirs = pl.ds(pl.multiple_of(((1 - hi) * 2 + core) * SHARD, SHARD), SHARD)
    passed = []
    for j, ref in enumerate((weight, bias)):
        copy = pltpu.make_async_remote_copy(
            src_ref=ref.at[theirs], dst_ref=ref.at[theirs], send_sem=w_send.at[4 + j], recv_sem=w_recv.at[4 + j],
            device_id=partner, device_id_type=MESH,
        )
        copy.start()
        passed.append(copy)
    shift_rows(2, 6, 4 * core, 4)
    for copy in weight_copies[2:] + passed:
        copy.wait_recv()
    keep_weight.wait()
    keep_bias.wait()
    do_pair(2 * core, 0)

    @pl.when(has_prev)
    def _():
        arrive_z(0)
        shift_rows(0, 2, 4 * core, 4)

    do_pair_z(2 * core, 0)

    arrive(1)

    def swap(lo, n, k):
        return pltpu.make_async_remote_copy(
            src_ref=taken.at[pl.ds(lo, n), 6 - 5 * core], dst_ref=taken.at[pl.ds(lo, n), 7 * core],
            send_sem=swap_send.at[k], recv_sem=swap_recv.at[k], device_id=partner, device_id_type=MESH,
        )

    swap(2, 4, 0).start()
    shift_rows(2, 6, 4 - 3 * core, 3)
    do_pair(1, 1)
    swap(2, 4, 0).wait_recv()

    @pl.loop(2, 6)
    def _(slot):
        shift(slot, 7 * (1 - core))

    do_pair(2 - 2 * core, 2)

    @pl.when(has_prev)
    def _():
        arrive_z(1)
        swap(0, 2, 1).start()
        shift_rows(0, 2, 4 - 3 * core, 3)

    do_pair_z(1, 1)

    @pl.when(has_prev)
    def _():
        swap(0, 2, 1).wait_recv()

        @pl.loop(0, 2)
        def _(slot):
            shift(slot, 7 * (1 - core))

    do_pair_z(2 - 2 * core, 2)

    pltpu.make_async_copy(back, back, out_recv).wait()

    @pl.loop(0, ROWS)
    def _(r):
        flat[pl.ds(pl.multiple_of(r * SHARD, SHARD), SHARD), :] = back[r].astype(jnp.float32)

    @pl.loop(0, SHARD)
    def _(c):
        temporal_rows = flat[pl.ds(c, ROWS, stride=SHARD), :]
        out_ref[c, 0] = (lat[c, :ROWS].astype(jnp.float32) + temporal_rows).astype(jnp.bfloat16)

    for copy in weight_copies + passed:
        copy.wait_send()
    for copy in in_copies:
        copy.wait_send()

    @pl.when(has_next)
    def _():
        for chunk in range(2):
            for sx in (2, 3):
                for sq in range(4):
                    z_copy(chunk, sx, sq).wait_send()

    swap(2, 4, 0).wait_send()

    @pl.when(has_prev)
    def _():
        swap(0, 2, 1).wait_send()

    for step, pair in ((0, 2 * core), (1, 1), (2, 2 - 2 * core)):
        @pl.loop(0, 4)
        def _(frame):
            each_home(frame, pair, step, lambda far: far.wait_send(), lambda src, dst: None)


def on_device(latents, space_weight, space_bias, time_weight, time_bias):
    weight = jnp.concatenate(
        [space_weight.reshape(SHARD, SPACE_K), time_weight.transpose(1, 0, 2).reshape(SHARD, TIME_K)], axis=1
    )
    bias = jnp.pad(jnp.stack([space_bias, time_bias], axis=1), ((0, 0), (0, COLS - 2)))
    vmem, dma = pltpu.VMEM, pltpu.SemaphoreType.DMA
    bf16, f32 = jnp.bfloat16, jnp.float32
    return pl.pallas_call(
        kernel,
        out_shape=jax.ShapeDtypeStruct(latents.shape, bf16),
        in_specs=[pl.BlockSpec(memory_space=pl.ANY)] * 3,
        out_specs=pl.BlockSpec(memory_space=pltpu.VMEM),
        scratch_shapes=[
            vmem((SHARD, PITCH, COLS), bf16),
            vmem((SHARD * PITCH, COLS), f32),
            vmem((ROWS + 2, SHARD, COLS), bf16),
            vmem((6, 8, CH, COLS), bf16),
            vmem((6, 8, CH, COLS), bf16),
            vmem((6, 8, CH, COLS), bf16),
            vmem((6, 6, CH, COLS), bf16),
            vmem((4, 6, CH, COLS), bf16),
            vmem((ROWS, SHARD, COLS), bf16),
            vmem((CH, SPACE_K + TIME_K), bf16),
            vmem((CH, COLS), f32),
            vmem((SHARD, SPACE_K + TIME_K), bf16),
            vmem((SHARD, COLS), f32),
            dma((6,)),
            dma((2, 15)),
            dma((2, 16)),
            dma((2, 8)),
            dma((2, 8)),
            dma((2,)),
            dma((2,)),
            dma((6,)),
            dma((6,)),
            dma((3, 4, 4)),
            dma,
        ],
        compiler_params=pltpu.CompilerParams(collective_id=0, has_side_effects=True, vmem_limit_bytes=56 << 20),
        cost_estimate=pl.CostEstimate(flops=6_000_000_000, bytes_accessed=6_000_000, transcendentals=1_200_000),
    )(latents, weight, bias)


def solution(mesh):
    return jax.shard_map(
        on_device,
        mesh=mesh,
        in_specs=(
            P("ch", "sp", None, None),
            P("ch", None, None),
            P("ch"),
            P(None, "ch", None),
            P("ch"),
        ),
        out_specs=P("ch", "sp", None, None),
        check_vma=False,
    )
```

time: 483 us -> 95.1 us (0.20)
  the two profiles are of different devices: /device:TPU:1 before, /device:TPU:65 now
where the time goes in v1:
time: 95.1 us; the launch traced here: 94.9 us
  Pallas kernels  85.5 us (90%)
  local copies, waits for them, and re-layouts  7.8 us (8%)
  other arithmetic  1.57 us (2%)
    pallas_call x1, Pallas kernels, on_device(): pl.pallas_call(kernel, out_shape=jax.ShapeDtypeStruct(latents.shape, bf16...  85.5 us
    pallas_call x1, local copies, waits for them, and re-layouts, on_device(): pl.pallas_call(kernel, out_shape=jax.ShapeDtypeStruct(latents.shape, bf16...  3.09 us
    unnamed x3, local copies, waits for them, and re-layouts  2.12 us

profile of v1, /device:TPU:65, one launch (start us, length us, event | category | flops | bytes accessed | tf_op | source)
XLA Modules:
  0.0 94.9 jit_solution(10010633675075791592)
XLA Ops:
  0.0 0.0 copy-start
  0.0 0.8 pad_maximum_fusion.1
  0.8 0.1 copy.20
  0.9 0.6 pad.4.bias_hbm
  1.5 0.9 copy.24
  2.4 1.0 %copy.23 = bf16[9,8,8,256]{3,2,0,1:T(8,128)(2,1)S(1)} copy(bf16[9,8,8,256]{3,2,1,0:T(8,128)(2,1)} %bitcast.9) | data formatting | bytes 589824 | tf_op jit(solution)/shard_map/reshape | solution.py:334
  3.4 0.8 pad_maximum_fusion.weight_hbm
  4.2 0.0 copy-done
  4.2 2.1 %copy.21.lat_hbm = bf16[64,1,90,128]{3,2,1,0:T(8,128)(2,1)} copy(bf16[64,1,90,128]{3,0,2,1:T(8,128)(2,1)S(1)} %copy-done) | data formatting | bytes 2949120 | tf_op args[0]
  6.3 85.5 %shard_map.55 = bf16[64,1,90,128]{3,2,1,0:T(8,128)(2,1)} custom-call(bf16[64,1,90,128]{3,2,1,0:T(8,128)(2,1)} %copy.21.lat_hbm, bf16[64,3072]{1,0:T(8,128)(2,1)} %pad_maximum_fusion.weight_hbm, f32[64,128]{1,0:T(8,128)} %pad.4.bias_hbm), custom_call_target="tpu_custom_call" | custom-call | flops 6000000000 | bytes 6000000 | tf_op jit(solution)/shard_map/pallas_call | solution.py:339
  91.8 3.1 %copy.22 = bf16[64,1,90,128]{3,0,2,1:T(8,128)(2,1)} copy(bf16[64,1,90,128]{3,2,1,0:T(8,128)(2,1)} %shard_map.55) | data formatting | bytes 2949120 | tf_op jit(solution)/shard_map/pallas_call | solution.py:339
Async XLA Ops:
  0.0 4.2 %copy-start = (bf16[64,1,90,128]{3,0,2,1:T(8,128)(2,1)S(1)}, bf16[64,1,90,128]{3,0,2,1:T(8,128)(2,1)}, u32[]{:S(2)}) copy-start(bf16[64,1,90,128]{3,0,2,1:T(8,128)(2,1)} %param.5) | copy-start | bytes 4423684

commit v2 on v1

--- a/solution.py
+++ b/solution.py
@@ -9,9 +9,7 @@
 
 MESH = pl.DeviceIdType.MESH
 ROWS, COLS, CH, SHARD = 90, 128, 256, 64
-PITCH = 96
 NZ = 8
-SPACE_K, TIME_K = 9 * CH, 3 * CH
 ORDER = ((1, 2), (3, 0), (2, 3), (0, 2), (1, 0), (3, 2), (2, 0), (0, 3), (1, 3), (3, 1), (2, 2), (1, 1), (3, 3), (2, 1), (0, 1))
 
 
@@ -20,8 +18,8 @@
 
 
 def kernel(
-    lat_hbm, weight_hbm, bias_hbm, out_ref,
-    lat, flat, sent, taken, left, right, hidden, made, back, weight, bias, own_weight, own_bias,
+    lat_hbm, space_hbm, time_hbm, space_bias, time_bias, back,
+    sent, taken, left, right, hidden, made, space, time, bias, own_space, own_time, own_bias,
     load_sem, in_send, in_recv, z_send, z_recv, swap_send, swap_recv, w_send, w_recv, out_send, out_recv,
 ):
     sp, q = lax.axis_index("sp"), lax.axis_index("ch")
@@ -33,8 +31,9 @@
     me = x * 4 + q
     has_prev = row_of_frames > 0
     has_next = row_of_frames < 2 * NZ - 1
-    start = chip_start(2 * x + hi)
-    short = lax.rem(2 * x + hi, 4) < 3
+    slab = 2 * x + lax.rem(hi + yh, 2)
+    start = chip_start(slab)
+    short = lax.rem(slab, 4) < 3
 
     def device(dx, fc):
         nx = lax.rem(x + dx, 4)
@@ -44,19 +43,21 @@
     def ident(nx, nq):
         return {"sp": base + nx, "ch": nq}
 
+    def along(step):
+        turns = z == (NZ - 1 if step > 0 else 0)
+        return {"sp": lax.rem(sp + 4 * step + 8 * NZ, 8 * NZ), "ch": jnp.where(turns, (1 - hi) * 2 + core, q)}
+
     partner = {"sp": sp, "ch": hi * 2 + 1 - core}
     across = {"sp": (1 - yh) * 4 * NZ + z * 4 + x, "ch": (1 - hi) * 2 + core}
 
-    loads = []
-    for part in range(4):
-        piece = pl.ds(part * 16, 16)
-        copy = pltpu.make_async_copy(lat_hbm.at[piece, 0], lat.at[piece, pl.ds(0, ROWS)], load_sem.at[part])
+    loads = [
+        pltpu.make_async_copy(src, dst, load_sem.at[i])
+        for i, (src, dst) in enumerate((
+            (lat_hbm, sent.at[pl.ds(1, ROWS)]), (space_hbm, own_space), (time_hbm, own_time),
+        ))
+    ]
+    for copy in loads:
         copy.start()
-        loads.append(copy)
-    load_weight = pltpu.make_async_copy(weight_hbm, own_weight, load_sem.at[4])
-    load_bias = pltpu.make_async_copy(bias_hbm, own_bias, load_sem.at[5])
-    load_weight.start()
-    load_bias.start()
     barrier = pltpu.get_barrier_semaphore()
     for dx, fc in ORDER:
         pl.semaphore_signal(barrier, inc=1, device_id=ident(*device(dx, fc)), device_id_type=MESH)
@@ -64,51 +65,50 @@
 
     @pl.when(has_prev)
     def _():
-        pl.semaphore_signal(barrier, inc=1, device_id={"sp": sp - 4, "ch": q}, device_id_type=MESH)
+        pl.semaphore_signal(barrier, inc=1, device_id=along(-1), device_id_type=MESH)
 
     sent[0] = jnp.zeros((SHARD, COLS), jnp.bfloat16)
     sent[ROWS + 1] = jnp.zeros((SHARD, COLS), jnp.bfloat16)
-    for part in range(4):
-        loads[part].wait()
-
-        @pl.loop(part * 16, part * 16 + 16)
-        def _(c):
-            flat[pl.ds(pl.multiple_of(c * PITCH, PITCH), PITCH), :] = lat[c].astype(jnp.float32)
-
-    @pl.loop(0, ROWS)
-    def _(r):
-        sent[r + 1] = flat[pl.ds(r, SHARD, stride=PITCH), :].astype(jnp.bfloat16)
-
+    at = lax.broadcasted_iota(jnp.int32, (SHARD, SHARD), 0) == lax.broadcasted_iota(jnp.int32, (SHARD, SHARD), 1)
+    for k, ref in enumerate((space_bias, time_bias)):
+        column = jnp.sum(jnp.where(at, ref[...], 0.0), axis=1, keepdims=True)
+        own_bias[:, k * SHARD:(k + 1) * SHARD] = jnp.broadcast_to(column, (SHARD, SHARD))
+    for copy in loads:
+        copy.wait()
     pl.semaphore_wait(barrier, 16 + has_next.astype(jnp.int32))
 
-    load_weight.wait()
-    load_bias.wait()
-    weight_rows = pl.ds(pl.multiple_of(q * SHARD, SHARD), SHARD)
+    def block(of):
+        return pl.ds(pl.multiple_of(of * SHARD, SHARD), SHARD)
+
+    parts = (
+        (own_space, lambda of: space.at[:, block(of)]),
+        (own_time, lambda of: time.at[:, block(of)]),
+        (own_bias, lambda of: bias.at[block(of)]),
+    )
     weight_copies = []
     for i, there in enumerate((across, partner)):
-        for j, (src, dst) in enumerate(((own_weight, weight), (own_bias, bias))):
+        for j, (src, dst) in enumerate(parts):
             copy = pltpu.make_async_remote_copy(
-                src_ref=src, dst_ref=dst.at[weight_rows], send_sem=w_send.at[2 * i + j], recv_sem=w_recv.at[2 * i + j],
+                src_ref=src, dst_ref=dst(q), send_sem=w_send.at[3 * i + j], recv_sem=w_recv.at[3 * i + j],
                 device_id=there, device_id_type=MESH,
             )
             copy.start()
             weight_copies.append(copy)
-    keep_weight = pltpu.make_async_copy(own_weight, weight.at[weight_rows], load_sem.at[4])
-    keep_bias = pltpu.make_async_copy(own_bias, bias.at[weight_rows], load_sem.at[5])
-    keep_weight.start()
-    keep_bias.start()
+    keeps = [pltpu.make_async_copy(src, dst(q), load_sem.at[j]) for j, (src, dst) in enumerate(parts)]
+    for copy in keeps:
+        copy.start()
 
     def in_piece(chunk, t_chip, t_core):
         if chunk == 0:
             return chip_start(t_chip) + 10 * t_core, 4 * t_core, 4
         return chip_start(t_chip) + 4 + 3 * t_core, 4 - 3 * t_core, 3
 
-    my_channels = pl.ds(pl.multiple_of(q * SHARD, SHARD), SHARD)
+    my_channels = block(q)
     in_copies = []
     for chunk in range(2):
         for k, (dx, fc) in enumerate(ORDER):
             nx, nq = device(dx, fc)
-            src, dst, n = in_piece(chunk, 2 * nx + nq // 2, lax.rem(nq, 2))
+            src, dst, n = in_piece(chunk, 2 * nx + lax.rem(nq // 2 + yh, 2), lax.rem(nq, 2))
             copy = pltpu.make_async_remote_copy(
                 src_ref=sent.at[pl.ds(src, n)], dst_ref=taken.at[2 + x, pl.ds(dst, n), my_channels],
                 send_sem=in_send.at[chunk, k], recv_sem=in_recv.at[chunk, me],
@@ -116,7 +116,7 @@
             )
             copy.start()
             in_copies.append(copy)
-        src, dst, n = in_piece(chunk, 2 * x + hi, core)
+        src, dst, n = in_piece(chunk, slab, core)
         pltpu.make_async_copy(
             sent.at[pl.ds(src, n)], taken.at[2 + x, pl.ds(dst, n), my_channels], in_recv.at[chunk, me]
         ).start()
@@ -127,7 +127,7 @@
             src_ref=taken.at[2 + sx, pl.ds(dst, n), pl.ds(sq * SHARD, SHARD)],
             dst_ref=taken.at[sx - 2, pl.ds(dst, n), pl.ds(sq * SHARD, SHARD)],
             send_sem=z_send.at[chunk, (sx - 2) * 4 + sq], recv_sem=z_recv.at[chunk, (sx - 2) * 4 + sq],
-            device_id={"sp": jnp.minimum(sp + 4, 8 * NZ - 1), "ch": q}, device_id_type=MESH,
+            device_id=along(1), device_id_type=MESH,
         )
 
     def arrive(chunk):
@@ -155,8 +155,8 @@
         for dy in range(3):
             for buf in (left, taken, right):
                 taps.append(jnp.concatenate([buf[slot, 2 * pair + dy], buf[slot, 2 * pair + dy + 1]], axis=1))
-        rhs = jnp.concatenate(taps, axis=0)
-        v = jnp.dot(weight[:, :SPACE_K], rhs, preferred_element_type=jnp.float32) + bias[:, 0:1]
+        lhs = jnp.concatenate([space[tap] for tap in range(9)], axis=1)
+        v = jnp.dot(lhs, jnp.concatenate(taps, axis=0), preferred_element_type=jnp.float32) + bias[:, 0:1]
         h = (v / (1.0 + jnp.exp(-v))).astype(jnp.bfloat16)
         hidden[slot, 2 * pair] = h[:, :COLS]
         hidden[slot, 2 * pair + 1] = h[:, COLS:]
@@ -166,8 +166,8 @@
             jnp.concatenate([hidden[frame + 2 - lag, 2 * pair], hidden[frame + 2 - lag, 2 * pair + 1]], axis=1)
             for lag in range(3)
         ]
-        rhs = jnp.concatenate(lags, axis=0)
-        v = jnp.dot(weight[:, SPACE_K:], rhs, preferred_element_type=jnp.float32) + bias[:, 1:2]
+        lhs = jnp.concatenate([time[lag] for lag in range(3)], axis=1)
+        v = jnp.dot(lhs, jnp.concatenate(lags, axis=0), preferred_element_type=jnp.float32) + bias[:, SHARD:SHARD + 1]
         y = v.astype(jnp.bfloat16)
         made[frame, 2 * pair] = y[:, :COLS]
         made[frame, 2 * pair + 1] = y[:, COLS:]
@@ -232,22 +232,22 @@
             shift(i // n, idx0 + lax.rem(i, n))
 
     arrive(0)
-    for copy in weight_copies[:2]:
+    for copy in weight_copies[:3]:
         copy.wait_recv()
-    theirs = pl.ds(pl.multiple_of(((1 - hi) * 2 + core) * SHARD, SHARD), SHARD)
+    theirs = (1 - hi) * 2 + core
     passed = []
-    for j, ref in enumerate((weight, bias)):
+    for j, (_, dst) in enumerate(parts):
         copy = pltpu.make_async_remote_copy(
-            src_ref=ref.at[theirs], dst_ref=ref.at[theirs], send_sem=w_send.at[4 + j], recv_sem=w_recv.at[4 + j],
+            src_ref=dst(theirs), dst_ref=dst(theirs), send_sem=w_send.at[6 + j], recv_sem=w_recv.at[6 + j],
             device_id=partner, device_id_type=MESH,
         )
         copy.start()
         passed.append(copy)
     shift_rows(2, 6, 4 * core, 4)
-    for copy in weight_copies[2:] + passed:
+    for copy in weight_copies[3:] + passed:
         copy.wait_recv()
-    keep_weight.wait()
-    keep_bias.wait()
+    for copy in keeps:
+        copy.wait()
     do_pair(2 * core, 0)
 
     @pl.when(has_prev)
@@ -296,15 +296,6 @@
 
     pltpu.make_async_copy(back, back, out_recv).wait()
 
-    @pl.loop(0, ROWS)
-    def _(r):
-        flat[pl.ds(pl.multiple_of(r * SHARD, SHARD), SHARD), :] = back[r].astype(jnp.float32)
-
-    @pl.loop(0, SHARD)
-    def _(c):
-        temporal_rows = flat[pl.ds(c, ROWS, stride=SHARD), :]
-        out_ref[c, 0] = (lat[c, :ROWS].astype(jnp.float32) + temporal_rows).astype(jnp.bfloat16)
-
     for copy in weight_copies + passed:
         copy.wait_send()
     for copy in in_copies:
@@ -330,46 +321,44 @@
 
 
 def on_device(latents, space_weight, space_bias, time_weight, time_bias):
-    weight = jnp.concatenate(
-        [space_weight.reshape(SHARD, SPACE_K), time_weight.transpose(1, 0, 2).reshape(SHARD, TIME_K)], axis=1
-    )
-    bias = jnp.pad(jnp.stack([space_bias, time_bias], axis=1), ((0, 0), (0, COLS - 2)))
+    rows_first = latents[:, 0].transpose(1, 0, 2)
     vmem, dma = pltpu.VMEM, pltpu.SemaphoreType.DMA
     bf16, f32 = jnp.bfloat16, jnp.float32
-    return pl.pallas_call(
+    temporal = pl.pallas_call(
         kernel,
-        out_shape=jax.ShapeDtypeStruct(latents.shape, bf16),
-        in_specs=[pl.BlockSpec(memory_space=pl.ANY)] * 3,
-        out_specs=pl.BlockSpec(memory_space=pltpu.VMEM),
+        out_shape=jax.ShapeDtypeStruct(rows_first.shape, bf16),
+        in_specs=[pl.BlockSpec(memory_space=pltpu.HBM)] * 3 + [pl.BlockSpec(memory_space=pltpu.VMEM)] * 2,
+        out_specs=pl.BlockSpec(memory_space=pl.ANY),
         scratch_shapes=[
-            vmem((SHARD, PITCH, COLS), bf16),
-            vmem((SHARD * PITCH, COLS), f32),
             vmem((ROWS + 2, SHARD, COLS), bf16),
             vmem((6, 8, CH, COLS), bf16),
             vmem((6, 8, CH, COLS), bf16),
             vmem((6, 8, CH, COLS), bf16),
             vmem((6, 6, CH, COLS), bf16),
             vmem((4, 6, CH, COLS), bf16),
-            vmem((ROWS, SHARD, COLS), bf16),
-            vmem((CH, SPACE_K + TIME_K), bf16),
+            vmem((9, CH, CH), bf16),
+            vmem((3, CH, CH), bf16),
             vmem((CH, COLS), f32),
-            vmem((SHARD, SPACE_K + TIME_K), bf16),
+            vmem((9, SHARD, CH), bf16),
+            vmem((3, SHARD, CH), bf16),
             vmem((SHARD, COLS), f32),
-            dma((6,)),
+            dma((4,)),
             dma((2, 15)),
             dma((2, 16)),
             dma((2, 8)),
             dma((2, 8)),
             dma((2,)),
             dma((2,)),
-            dma((6,)),
-            dma((6,)),
+            dma((9,)),
+            dma((9,)),
             dma((3, 4, 4)),
             dma,
         ],
-        compiler_params=pltpu.CompilerParams(collective_id=0, has_side_effects=True, vmem_limit_bytes=56 << 20),
+        compiler_params=pltpu.CompilerParams(collective_id=0, has_side_effects=True, vmem_limit_bytes=62 << 20),
         cost_estimate=pl.CostEstimate(flops=6_000_000_000, bytes_accessed=6_000_000, transcendentals=1_200_000),
-    )(latents, weight, bias)
+    )(rows_first, space_weight.transpose(1, 0, 2), time_weight, space_bias[None], time_bias[None])
+    total = rows_first.astype(f32) + temporal.astype(f32)
+    return total.astype(bf16).transpose(1, 0, 2)[:, None]
 
 
 def solution(mesh):

time: 95.1 us -> 63.2 us (0.66)
  the two profiles are of different devices: /device:TPU:65 before, /device:TPU:25 now
where the time goes in v2:
time: 63.2 us; the launch traced here: 62.6 us
  Pallas kernels  59.5 us (94%)
  other arithmetic  3.1 us (5%)
    pallas_call x1, Pallas kernels, on_device(): pl.pallas_call(kernel, out_shape=jax.ShapeDtypeStruct(rows_first.shape, b...  59.5 us
    broadcast_in_dim x1, other arithmetic, on_device(): return total.astype(bf16).transpose(1, 0, 2)[:, None]  3.1 us

profile of v2, /device:TPU:25, one launch (start us, length us, event | category | flops | bytes accessed | tf_op | source)
XLA Modules:
  0.0 62.6 jit_solution(16000680087788529559)
XLA Ops:
  0.0 0.0 copy-start
  0.0 59.5 %shard_map.55 = bf16[90,64,128]{2,1,0:T(8,128)(2,1)} custom-call(bf16[90,64,128]{2,1,0:T(8,128)(2,1)} %bitcast.11, bf16[9,64,256]{2,1,0:T(8,128)(2,1)} %bitcast.12, bf16[3,64,256]{2,1,0:T(8,128)(2,1)} %time_hbm.1, f32[1,64]{1,0:T(1,128)} %bitcast.13, f32[1,64]{1,0:T(1,128)} %bitcast.14), custom_call_target="tpu_custom_call" | custom-call | flops 6000000000 | bytes 6000000 | tf_op jit(solution)/shard_map/pallas_call | solution.py:327
  59.5 0.0 copy-done
  59.5 3.1 %fusion = bf16[64,1,90,128]{3,0,2,1:T(8,128)(2,1)} fusion(bf16[90,64,128]{2,1,0:T(8,128)(2,1)} %shard_map.55, bf16[64,1,90,128]{3,0,2,1:T(8,128)(2,1)S(1)} %copy-done), kind=kLoop, calls=%fused_computation.1 | loop fusion | flops 2949120 | bytes 4423680 | tf_op jit(solution)/shard_map/broadcast_in_dim | solution.py:361
Async XLA Ops:
  0.0 59.5 %copy-start = (bf16[64,1,90,128]{3,0,2,1:T(8,128)(2,1)S(1)}, bf16[64,1,90,128]{3,0,2,1:T(8,128)(2,1)}, u32[]{:S(2)}) copy-start(bf16[64,1,90,128]{3,0,2,1:T(8,128)(2,1)} %param.5) | copy-start | bytes 4423684

commit v3 on v2

--- a/solution.py
+++ b/solution.py
@@ -17,9 +17,13 @@
     return (45 * chip) // 4
 
 
+def chunk_start(chip, core):
+    return chip_start(chip) + 6 * core
+
+
 def kernel(
     lat_hbm, space_hbm, time_hbm, space_bias, time_bias, back,
-    sent, taken, left, right, hidden, made, space, time, bias, own_space, own_time, own_bias,
+    sent, taken, hidden, made, space, time, bias, own_space, own_time, own_bias,
     load_sem, in_send, in_recv, z_send, z_recv, swap_send, swap_recv, w_send, w_recv, out_send, out_recv,
 ):
     sp, q = lax.axis_index("sp"), lax.axis_index("ch")
@@ -98,66 +102,76 @@
     for copy in keeps:
         copy.start()
 
-    def in_piece(chunk, t_chip, t_core):
-        if chunk == 0:
-            return chip_start(t_chip) + 10 * t_core, 4 * t_core, 4
-        return chip_start(t_chip) + 4 + 3 * t_core, 4 - 3 * t_core, 3
+    chunk_rows = (4, 2, 1)
+
+    def chunk_at(chunk, of_core):
+        return (4 * of_core, 4 - 2 * of_core, 6 - 5 * of_core)[chunk]
 
     my_channels = block(q)
+    def in_source(chunk, t_slab, t_core):
+        return sent.at[pl.ds(chunk_start(t_slab, t_core) + chunk_at(chunk, t_core), chunk_rows[chunk])]
+
+    def in_target(chunk, slot, of_core, channels):
+        return taken.at[slot, pl.ds(chunk_at(chunk, of_core), chunk_rows[chunk]), channels]
+
     in_copies = []
-    for chunk in range(2):
+    for chunk in range(3):
+        pltpu.make_async_copy(
+            in_source(chunk, slab, core), in_target(chunk, 2 + x, core, my_channels), in_recv.at[chunk, me]
+        ).start()
         for k, (dx, fc) in enumerate(ORDER):
             nx, nq = device(dx, fc)
-            src, dst, n = in_piece(chunk, 2 * nx + lax.rem(nq // 2 + yh, 2), lax.rem(nq, 2))
+            t_core = lax.rem(nq, 2)
             copy = pltpu.make_async_remote_copy(
-                src_ref=sent.at[pl.ds(src, n)], dst_ref=taken.at[2 + x, pl.ds(dst, n), my_channels],
+                src_ref=in_source(chunk, 2 * nx + lax.rem(nq // 2 + yh, 2), t_core),
+                dst_ref=in_target(chunk, 2 + x, t_core, my_channels),
                 send_sem=in_send.at[chunk, k], recv_sem=in_recv.at[chunk, me],
                 device_id=ident(nx, nq), device_id_type=MESH,
             )
             copy.start()
             in_copies.append(copy)
-        src, dst, n = in_piece(chunk, slab, core)
-        pltpu.make_async_copy(
-            sent.at[pl.ds(src, n)], taken.at[2 + x, pl.ds(dst, n), my_channels], in_recv.at[chunk, me]
-        ).start()
-
-    def z_copy(chunk, sx, sq):
-        _, dst, n = in_piece(chunk, 0, core)
+
+    def z_copy(chunk, frame, sq):
         return pltpu.make_async_remote_copy(
-            src_ref=taken.at[2 + sx, pl.ds(dst, n), pl.ds(sq * SHARD, SHARD)],
-            dst_ref=taken.at[sx - 2, pl.ds(dst, n), pl.ds(sq * SHARD, SHARD)],
-            send_sem=z_send.at[chunk, (sx - 2) * 4 + sq], recv_sem=z_recv.at[chunk, (sx - 2) * 4 + sq],
+            src_ref=in_target(chunk, 4 + frame, core, block(sq)), dst_ref=in_target(chunk, frame, core, block(sq)),
+            send_sem=z_send.at[chunk, frame * 4 + sq], recv_sem=z_recv.at[chunk, frame * 4 + sq],
             device_id=along(1), device_id_type=MESH,
         )
 
     def arrive(chunk):
-        _, dst, n = in_piece(chunk, 0, core)
-        for sx in (2, 3, 0, 1):
+        for dx, fc in ((0, 0),) + ORDER:
+            sx, sq = lax.rem(x + 4 - dx, 4), device(dx, fc)[1]
+            got = in_target(chunk, 2 + sx, core, block(sq))
+            pltpu.make_async_copy(got, got, in_recv.at[chunk, sx * 4 + sq]).wait()
+
+            @pl.when(jnp.logical_and(has_next, sx >= 2))
+            def _():
+                z_copy(chunk, sx - 2, sq).start()
+
+    def arrive_z(chunk):
+        for frame in range(2):
             for sq in range(4):
-                got = taken.at[2 + sx, pl.ds(dst, n), pl.ds(sq * SHARD, SHARD)]
-                pltpu.make_async_copy(got, got, in_recv.at[chunk, sx * 4 + sq]).wait()
-                if sx >= 2:
-                    pl.when(has_next)(lambda sx=sx, sq=sq: z_copy(chunk, sx, sq).start())
-
-    def arrive_z(chunk):
-        for sx in (2, 3):
-            for sq in range(4):
-                z_copy(chunk, sx, sq).wait_recv()
-
-    def shift(slot, idx):
-        row = taken[slot, idx].astype(jnp.float32)
-        lane = lax.broadcasted_iota(jnp.int32, row.shape, 1)
-        left[slot, idx] = jnp.where(lane == 0, 0.0, pltpu.roll(row, 1, 1)).astype(jnp.bfloat16)
-        right[slot, idx] = jnp.where(lane == COLS - 1, 0.0, pltpu.roll(row, COLS - 1, 1)).astype(jnp.bfloat16)
+                z_copy(chunk, frame, sq).wait_recv()
+
+    lane = lax.broadcasted_iota(jnp.int32, (CH, COLS), 1)
+    first_lane, last_lane = lane == 0, lane == COLS - 1
 
     def conv(slot, pair):
-        taps = []
-        for dy in range(3):
-            for buf in (left, taken, right):
-                taps.append(jnp.concatenate([buf[slot, 2 * pair + dy], buf[slot, 2 * pair + dy + 1]], axis=1))
+        rows = []
+        for k in range(4):
+            row = taken[slot, 2 * pair + k]
+            zero = jnp.zeros_like(row)
+            rows.append((
+                jnp.where(first_lane, zero, pltpu.roll(row, 1, 1)), row,
+                jnp.where(last_lane, zero, pltpu.roll(row, COLS - 1, 1)),
+            ))
+        taps = [
+            jnp.concatenate([rows[dy][dx], rows[dy + 1][dx]], axis=1) for dy in range(3) for dx in range(3)
+        ]
         lhs = jnp.concatenate([space[tap] for tap in range(9)], axis=1)
         v = jnp.dot(lhs, jnp.concatenate(taps, axis=0), preferred_element_type=jnp.float32) + bias[:, 0:1]
-        h = (v / (1.0 + jnp.exp(-v))).astype(jnp.bfloat16)
+        half = 0.5 * v
+        h = (half + half * jnp.tanh(half)).astype(jnp.bfloat16)
         hidden[slot, 2 * pair] = h[:, :COLS]
         hidden[slot, 2 * pair + 1] = h[:, COLS:]
 
@@ -197,39 +211,11 @@
             lambda src, dst: pltpu.make_async_copy(src, dst, out_recv).start(),
         )
 
-    def do_pair(pair, step):
-        @pl.loop(2, 6)
-        def _(slot):
-            conv(slot, pair)
-
-        @pl.loop(2, 4)
-        def _(frame):
-            temporal(frame, pair)
-            go_home(frame, pair, step)
-
-    def do_pair_z(pair, step):
-        @pl.when(has_prev)
-        def _():
-            @pl.loop(0, 2)
-            def _(slot):
-                conv(slot, pair)
-
-        @pl.when(jnp.logical_not(has_prev))
-        def _():
-            zero = jnp.zeros((CH, COLS), jnp.bfloat16)
-            for slot in range(2):
-                for k in range(2):
-                    hidden[slot, 2 * pair + k] = zero
-
-        @pl.loop(0, 2)
-        def _(frame):
-            temporal(frame, pair)
-            go_home(frame, pair, step)
-
-    def shift_rows(lo, hi_, idx0, n):
-        @pl.loop(lo * n, hi_ * n)
-        def _(i):
-            shift(i // n, idx0 + lax.rem(i, n))
+    def swap(lo, n, k):
+        return pltpu.make_async_remote_copy(
+            src_ref=taken.at[pl.ds(lo, n), 6 - 5 * core], dst_ref=taken.at[pl.ds(lo, n), 7 * core],
+            send_sem=swap_send.at[k], recv_sem=swap_recv.at[k], device_id=partner, device_id_type=MESH,
+        )
 
     arrive(0)
     for copy in weight_copies[:3]:
@@ -243,56 +229,57 @@
         )
         copy.start()
         passed.append(copy)
-    shift_rows(2, 6, 4 * core, 4)
     for copy in weight_copies[3:] + passed:
         copy.wait_recv()
     for copy in keeps:
         copy.wait()
-    do_pair(2 * core, 0)
-
-    @pl.when(has_prev)
-    def _():
-        arrive_z(0)
-        shift_rows(0, 2, 4 * core, 4)
-
-    do_pair_z(2 * core, 0)
-
-    arrive(1)
-
-    def swap(lo, n, k):
-        return pltpu.make_async_remote_copy(
-            src_ref=taken.at[pl.ds(lo, n), 6 - 5 * core], dst_ref=taken.at[pl.ds(lo, n), 7 * core],
-            send_sem=swap_send.at[k], recv_sem=swap_recv.at[k], device_id=partner, device_id_type=MESH,
-        )
-
-    swap(2, 4, 0).start()
-    shift_rows(2, 6, 4 - 3 * core, 3)
-    do_pair(1, 1)
-    swap(2, 4, 0).wait_recv()
-
-    @pl.loop(2, 6)
-    def _(slot):
-        shift(slot, 7 * (1 - core))
-
-    do_pair(2 - 2 * core, 2)
-
-    @pl.when(has_prev)
-    def _():
-        arrive_z(1)
-        swap(0, 2, 1).start()
-        shift_rows(0, 2, 4 - 3 * core, 3)
-
-    do_pair_z(1, 1)
-
-    @pl.when(has_prev)
-    def _():
-        swap(0, 2, 1).wait_recv()
-
-        @pl.loop(0, 2)
-        def _(slot):
-            shift(slot, 7 * (1 - core))
-
-    do_pair_z(2 - 2 * core, 2)
+
+    @pl.loop(0, 3)
+    def _(step):
+        pair = 2 * core + step * (1 - 2 * core)
+
+        @pl.when(step == 2)
+        def _():
+            swap(2, 4, 0).wait_recv()
+
+        for slot in range(2, 6):
+            conv(slot, pair)
+        for frame in (2, 3):
+            temporal(frame, pair)
+        for frame in (2, 3):
+            go_home(frame, pair, step)
+
+        for chunk in (1, 2):
+            @pl.when(step == chunk - 1)
+            def _():
+                arrive(chunk)
+                if chunk == 2:
+                    swap(2, 4, 0).start()
+
+        @pl.when(has_prev)
+        def _():
+            for chunk in range(3):
+                @pl.when(step == chunk)
+                def _():
+                    arrive_z(chunk)
+                    if chunk == 2:
+                        swap(0, 2, 1).start()
+                        swap(0, 2, 1).wait_recv()
+
+            for slot in range(2):
+                conv(slot, pair)
+
+        @pl.when(jnp.logical_not(has_prev))
+        def _():
+            zero = jnp.zeros((CH, COLS), jnp.bfloat16)
+            for slot in range(2):
+                for k in range(2):
+                    hidden[slot, 2 * pair + k] = zero
+
+        for frame in range(2):
+            temporal(frame, pair)
+        for frame in range(2):
+            go_home(frame, pair, step)
 
     pltpu.make_async_copy(back, back, out_recv).wait()
 
@@ -303,10 +290,10 @@
 
     @pl.when(has_next)
     def _():
-        for chunk in range(2):
-            for sx in (2, 3):
+        for chunk in range(3):
+            for frame in range(2):
                 for sq in range(4):
-                    z_copy(chunk, sx, sq).wait_send()
+                    z_copy(chunk, frame, sq).wait_send()
 
     swap(2, 4, 0).wait_send()
 
@@ -314,10 +301,12 @@
     def _():
         swap(0, 2, 1).wait_send()
 
-    for step, pair in ((0, 2 * core), (1, 1), (2, 2 - 2 * core)):
-        @pl.loop(0, 4)
-        def _(frame):
-            each_home(frame, pair, step, lambda far: far.wait_send(), lambda src, dst: None)
+    @pl.loop(0, 3)
+    def _(step):
+        for frame in range(4):
+            each_home(
+                frame, 2 * core + step * (1 - 2 * core), step, lambda far: far.wait_send(), lambda src, dst: None
+            )
 
 
 def on_device(latents, space_weight, space_bias, time_weight, time_bias):
@@ -332,8 +321,6 @@
         scratch_shapes=[
             vmem((ROWS + 2, SHARD, COLS), bf16),
             vmem((6, 8, CH, COLS), bf16),
-            vmem((6, 8, CH, COLS), bf16),
-            vmem((6, 8, CH, COLS), bf16),
             vmem((6, 6, CH, COLS), bf16),
             vmem((4, 6, CH, COLS), bf16),
             vmem((9, CH, CH), bf16),
@@ -343,10 +330,10 @@
             vmem((3, SHARD, CH), bf16),
             vmem((SHARD, COLS), f32),
             dma((4,)),
-            dma((2, 15)),
-            dma((2, 16)),
-            dma((2, 8)),
-            dma((2, 8)),
+            dma((3, 15)),
+            dma((3, 16)),
+            dma((3, 8)),
+            dma((3, 8)),
             dma((2,)),
             dma((2,)),
             dma((9,)),

time: 63.2 us -> 54.8 us (0.87)
  Pallas kernels: 59.5 us -> 51.3 us
    pallas_call x1, Pallas kernels: 59.5 us -> 51.3 us  [on_device(): pl.pallas_call(kernel, out_shape=jax.ShapeDtypeStruct(rows_first.shape, b...]
where the time goes in v3:
time: 54.8 us; the launch traced here: 54.4 us
  Pallas kernels  51.3 us (94%)
  other arithmetic  3.1 us (6%)
    pallas_call x1, Pallas kernels, on_device(): pl.pallas_call(kernel, out_shape=jax.ShapeDtypeStruct(rows_first.shape, b...  51.3 us
    broadcast_in_dim x1, other arithmetic, on_device(): return total.astype(bf16).transpose(1, 0, 2)[:, None]  3.1 us

profile of v3, /device:TPU:25, one launch (start us, length us, event | category | flops | bytes accessed | tf_op | source)
XLA Modules:
  0.0 54.4 jit_solution(9989392961441641073)
XLA Ops:
  0.0 0.0 copy-start
  0.0 51.3 %shard_map.55 = bf16[90,64,128]{2,1,0:T(8,128)(2,1)} custom-call(bf16[90,64,128]{2,1,0:T(8,128)(2,1)} %bitcast.11, bf16[9,64,256]{2,1,0:T(8,128)(2,1)} %bitcast.12, bf16[3,64,256]{2,1,0:T(8,128)(2,1)} %time_hbm.1, f32[1,64]{1,0:T(1,128)} %bitcast.13, f32[1,64]{1,0:T(1,128)} %bitcast.14), custom_call_target="tpu_custom_call" | custom-call | flops 6000000000 | bytes 6000000 | tf_op jit(solution)/shard_map/pallas_call | solution.py:316
  51.3 0.0 copy-done
  51.3 3.1 %fusion = bf16[64,1,90,128]{3,0,2,1:T(8,128)(2,1)} fusion(bf16[90,64,128]{2,1,0:T(8,128)(2,1)} %shard_map.55, bf16[64,1,90,128]{3,0,2,1:T(8,128)(2,1)S(1)} %copy-done), kind=kLoop, calls=%fused_computation.1 | loop fusion | flops 2949120 | bytes 4423680 | tf_op jit(solution)/shard_map/broadcast_in_dim | solution.py:348
Async XLA Ops:
  0.0 51.3 %copy-start = (bf16[64,1,90,128]{3,0,2,1:T(8,128)(2,1)S(1)}, bf16[64,1,90,128]{3,0,2,1:T(8,128)(2,1)}, u32[]{:S(2)}) copy-start(bf16[64,1,90,128]{3,0,2,1:T(8,128)(2,1)} %param.5) | copy-start | bytes 4423684

commit v4 on v3

v4 whole, which is shorter than its diff:
```python
import functools

import jax
import jax.numpy as jnp
from jax import lax
from jax.experimental import pallas as pl
from jax.experimental.pallas import tpu as pltpu
from jax.sharding import PartitionSpec as P

MESH = pl.DeviceIdType.MESH
ROWS, COLS, CH, SHARD = 90, 128, 256, 64
NZ = 8
ORDER = ((1, 2), (3, 0), (2, 3), (0, 2), (1, 0), (3, 2), (2, 0), (0, 3), (1, 3), (3, 1), (2, 2), (1, 1), (3, 3), (2, 1), (0, 1))


CHUNKS = ((2, 0, 3, 1), (2, 0, 5, 3), (2, 1, 1, 5), (1, 2, 0, 7))
EDGE = len(CHUNKS) - 1


def chip_start(chip):
    return (45 * chip) // 4


def chunk_start(chip, core):
    return chip_start(chip) + 6 * core


def kernel(
    lat_hbm, space_hbm, time_hbm, space_bias, time_bias, back,
    taken, hidden, made, space, time, bias, own_bias, raw_bias,
    keep_sem, in_send, in_recv, z_send, z_recv, swap_send, swap_recv, w_send, w_recv, out_send, out_recv,
):
    sp, q = lax.axis_index("sp"), lax.axis_index("ch")
    x = lax.rem(sp, 4)
    row_of_frames = sp // 4
    base = row_of_frames * 4
    z, yh = lax.rem(row_of_frames, NZ), row_of_frames // NZ
    hi, core = q // 2, lax.rem(q, 2)
    me = x * 4 + q
    has_prev = row_of_frames > 0
    has_next = row_of_frames < 2 * NZ - 1
    slab = 2 * x + lax.rem(hi + yh, 2)
    start = chip_start(slab)
    short = lax.rem(slab, 4) < 3

    def device(dx, fc):
        nx = lax.rem(x + dx, 4)
        nq = lax.rem(hi + fc // 2, 2) * 2 + lax.rem(core + fc % 2, 2)
        return nx, nq

    def ident(nx, nq):
        return {"sp": base + nx, "ch": nq}

    def along(step):
        turns = z == (NZ - 1 if step > 0 else 0)
        return {"sp": lax.rem(sp + 4 * step + 8 * NZ, 8 * NZ), "ch": jnp.where(turns, (1 - hi) * 2 + core, q)}

    crosses, relays, skips = row_of_frames == NZ, row_of_frames == 2 * NZ - 1, row_of_frames == 0
    ring_end = {"sp": 4 * (2 * NZ - 1) + x, "ch": q}
    ring_start = {"sp": 4 * NZ + x, "ch": q}
    partner = {"sp": sp, "ch": hi * 2 + 1 - core}
    across = {"sp": (1 - yh) * 4 * NZ + z * 4 + x, "ch": (1 - hi) * 2 + core}

    bias_loads = [
        pltpu.make_async_copy(src, raw_bias.at[k], keep_sem.at[4 + k]) for k, src in enumerate((space_bias, time_bias))
    ]
    for copy in bias_loads:
        copy.start()

    barrier = pltpu.get_barrier_semaphore()
    for dx, fc in ORDER:
        pl.semaphore_signal(barrier, inc=1, device_id=ident(*device(dx, fc)), device_id_type=MESH)
    pl.semaphore_signal(barrier, inc=1, device_id=across, device_id_type=MESH)

    @pl.when(has_prev)
    def _():
        pl.semaphore_signal(barrier, inc=1, device_id=along(-1), device_id_type=MESH)

    def has_edge(of_slab, of_core):
        return jnp.where(of_core == 0, of_slab != 0, of_slab == 3)

    edge = has_edge(slab, core)

    @pl.when(jnp.logical_not(edge))
    def _():
        for slot in range(6):
            taken[slot, 7 * core] = jnp.zeros((CH, COLS), jnp.bfloat16)

    @pl.when(crosses)
    def _():
        pl.semaphore_signal(barrier, inc=1, device_id=ring_end, device_id_type=MESH)

    pl.semaphore_wait(barrier, 17)

    def block(of):
        return pl.ds(pl.multiple_of(of * SHARD, SHARD), SHARD)

    parts = (
        (space_hbm.at[pl.ds(0, 6)], lambda of: space.at[pl.ds(0, 6), block(of)]),
        (space_hbm.at[pl.ds(6, 3)], lambda of: space.at[pl.ds(6, 3), block(of)]),
        (time_hbm, lambda of: time.at[:, block(of)]),
        (own_bias, lambda of: bias.at[block(of)]),
    )
    def weight_copy(j, of, there, k):
        src, dst = parts[j]
        return pltpu.make_async_remote_copy(
            src_ref=src if k < 8 else dst(of), dst_ref=dst(of), send_sem=w_send.at[k], recv_sem=w_recv.at[k % 12],
            device_id=there, device_id_type=MESH,
        )

    keeps = [pltpu.make_async_copy(src, dst(q), keep_sem.at[j]) for j, (src, dst) in enumerate(parts)]
    theirs = (1 - hi) * 2 + core

    def send_weight(j):
        if j == 0:
            pl.when(jnp.logical_not(skips))(weight_copy(j, q, across, j).start)
        else:
            weight_copy(j, q, across, j).start()
        weight_copy(j, q, partner, 4 + j).start()
        keeps[j].start()

    my_channels = block(q)

    def chunk_at(chunk, of_core):
        _, _, low, high = CHUNKS[chunk]
        return low + (high - low) * of_core

    def in_source(chunk, t_slab, t_core):
        first = chip_start(t_slab) - 1 + 6 * t_core + chunk_at(chunk, t_core)
        return lat_hbm.at[pl.ds(first, CHUNKS[chunk][0])]

    def in_target(chunk, slot, of_core, channels):
        return taken.at[slot, pl.ds(chunk_at(chunk, of_core), CHUNKS[chunk][0]), channels]

    in_copies = []
    for chunk in range(len(CHUNKS)):
        if chunk == 1:
            for j in range(3):
                send_weight(j)
        pl.when(jnp.logical_or(chunk < EDGE, edge))(
            pltpu.make_async_copy(
                in_source(chunk, slab, core), in_target(chunk, 2 + x, core, my_channels), in_recv.at[chunk, me]
            ).start
        )
        for k, (dx, fc) in enumerate(ORDER):
            nx, nq = device(dx, fc)
            t_slab, t_core = 2 * nx + lax.rem(nq // 2 + yh, 2), lax.rem(nq, 2)
            copy = pltpu.make_async_remote_copy(
                src_ref=in_source(chunk, t_slab, t_core),
                dst_ref=in_target(chunk, 2 + x, t_core, my_channels),
                send_sem=in_send.at[chunk, k], recv_sem=in_recv.at[chunk, me],
                device_id=ident(nx, nq), device_id_type=MESH,
            )
            sends = jnp.logical_or(chunk < EDGE, has_edge(t_slab, t_core))
            pl.when(sends)(copy.start)
            in_copies.append((sends, copy))

    for copy in bias_loads:
        copy.wait()
    raw_bias_rows = [raw_bias[0], raw_bias[1]]
    at = lax.broadcasted_iota(jnp.int32, (SHARD, SHARD), 0) == lax.broadcasted_iota(jnp.int32, (SHARD, SHARD), 1)
    for k, ref in enumerate(raw_bias_rows):
        column = jnp.sum(jnp.where(at, ref, 0.0), axis=1, keepdims=True)
        own_bias[:, k * SHARD:(k + 1) * SHARD] = jnp.broadcast_to(column, (SHARD, SHARD))
    send_weight(3)

    def z_copy(chunk, frame, sq):
        return pltpu.make_async_remote_copy(
            src_ref=in_target(chunk, 4 + frame, core, block(sq)), dst_ref=in_target(chunk, frame, core, block(sq)),
            send_sem=z_send.at[chunk, frame * 4 + sq], recv_sem=z_recv.at[chunk, frame * 4 + sq],
            device_id=along(1), device_id_type=MESH,
        )

    def step_chunks(step):
        return [chunk for chunk in range(len(CHUNKS)) if CHUNKS[chunk][1] == step]

    def arrive(step):
        for chunk in step_chunks(step):
            pl.when(jnp.logical_or(chunk < EDGE, edge))(functools.partial(arrive_chunk, chunk))

    def arrive_chunk(chunk):
        for dx, fc in ((0, 0),) + ORDER:
            sx, sq = lax.rem(x + 4 - dx, 4), device(dx, fc)[1]
            got = in_target(chunk, 2 + sx, core, block(sq))
            pltpu.make_async_copy(got, got, in_recv.at[chunk, sx * 4 + sq]).wait()

            @pl.when(jnp.logical_and(has_next, sx >= 2))
            def _():
                z_copy(chunk, sx - 2, sq).start()

    def arrive_z(step):
        for chunk in step_chunks(step):
            @pl.when(jnp.logical_or(chunk < EDGE, edge))
            def _():
                for frame in range(2):
                    for sq in range(4):
                        z_copy(chunk, frame, sq).wait_recv()

    lane = lax.broadcasted_iota(jnp.int32, (CH, COLS), 1)
    first_lane, last_lane = lane == 0, lane == COLS - 1

    def conv(slot, pair):
        rows = []
        for k in range(4):
            row = taken[slot, 2 * pair + k]
            zero = jnp.zeros_like(row)
            rows.append((
                jnp.where(first_lane, zero, pltpu.roll(row, 1, 1)), row,
                jnp.where(last_lane, zero, pltpu.roll(row, COLS - 1, 1)),
            ))
        taps = [
            jnp.concatenate([rows[dy][dx], rows[dy + 1][dx]], axis=1) for dy in range(3) for dx in range(3)
        ]
        lhs = jnp.concatenate([space[tap] for tap in range(9)], axis=1)
        v = jnp.dot(lhs, jnp.concatenate(taps, axis=0), preferred_element_type=jnp.float32) + bias[:, 0:1]
        half = 0.5 * v
        h = (half + half * jnp.tanh(half)).astype(jnp.bfloat16)
        hidden[slot, 2 * pair] = h[:, :COLS]
        hidden[slot, 2 * pair + 1] = h[:, COLS:]

    def temporal(frame, pair):
        lags = [
            jnp.concatenate([hidden[frame + 2 - lag, 2 * pair], hidden[frame + 2 - lag, 2 * pair + 1]], axis=1)
            for lag in range(3)
        ]
        lhs = jnp.concatenate([time[lag] for lag in range(3)], axis=1)
        v = jnp.dot(lhs, jnp.concatenate(lags, axis=0), preferred_element_type=jnp.float32) + bias[:, SHARD:SHARD + 1]
        y = v.astype(jnp.bfloat16).astype(jnp.float32)
        for k in range(2):
            own = taken[frame + 2, 2 * pair + 1 + k].astype(jnp.float32)
            made[frame, 2 * pair + k] = (own + y[:, k * COLS:(k + 1) * COLS]).astype(jnp.bfloat16)

    first_row = start + 6 * core

    def home_copy(frame, tq, pair, step, n):
        src = made.at[frame, pl.ds(2 * pair, n), pl.ds(pl.multiple_of(tq * SHARD, SHARD), SHARD)]
        dst = back.at[pl.ds(first_row + 2 * pair, n)]
        return src, dst, pltpu.make_async_remote_copy(
            src_ref=src, dst_ref=dst, send_sem=out_send.at[step, frame, tq], recv_sem=out_recv,
            device_id={"sp": base + frame, "ch": tq}, device_id_type=MESH,
        )

    def each_home(frame, pair, step, act_far, act_self):
        lacks = jnp.logical_and(jnp.logical_and(core == 1, short), pair == 2)
        for tq in range(4):
            is_me = jnp.logical_and(frame == x, tq == q)
            for n, fits in ((2, jnp.logical_not(lacks)), (1, lacks)):
                src, dst, far = home_copy(frame, tq, pair, step, n)
                pl.when(jnp.logical_and(fits, jnp.logical_not(is_me)))(functools.partial(act_far, far))
                pl.when(jnp.logical_and(fits, is_me))(functools.partial(act_self, src, dst))

    def go_home(frame, pair, step):
        each_home(
            frame, pair, step, lambda far: far.start(),
            lambda src, dst: pltpu.make_async_copy(src, dst, out_recv).start(),
        )

    def swap(lo, n, k):
        return pltpu.make_async_remote_copy(
            src_ref=taken.at[pl.ds(lo, n), 6 - 5 * core], dst_ref=taken.at[pl.ds(lo, n), 7 * core],
            send_sem=swap_send.at[k], recv_sem=swap_recv.at[k], device_id=partner, device_id_type=MESH,
        )

    @pl.when(relays)
    def _():
        weight_copy(0, q, across, 0).wait_recv()
        weight_copy(0, theirs, ring_start, 12).start()

    arrive(0)
    swap(2, 4, 0).start()
    pl.when(jnp.logical_not(relays))(weight_copy(0, q, across, 0).wait_recv)
    for j in range(4):
        if j > 0:
            weight_copy(j, q, across, j).wait_recv()
        weight_copy(j, theirs, partner, 8 + j).start()
    for j in range(4):
        weight_copy(j, q, partner, 4 + j).wait_recv()
        weight_copy(j, theirs, partner, 8 + j).wait_recv()
        keeps[j].wait()
    swap(2, 4, 0).wait_recv()

    def pair_of(step):
        return 2 * (1 - core) + step * (2 * core - 1)

    @pl.loop(0, 3)
    def _(step):
        pair = pair_of(step)

        for slot in range(2, 6):
            conv(slot, pair)
        for frame in (2, 3):
            temporal(frame, pair)
        for frame in (2, 3):
            go_home(frame, pair, step)

        for later in (1, 2):
            pl.when(step == later - 1)(functools.partial(arrive, later))

        @pl.when(has_prev)
        def _():
            for now in range(3):
                @pl.when(step == now)
                def _():
                    arrive_z(now)
                    if now == 0:
                        swap(0, 2, 1).start()
                        swap(0, 2, 1).wait_recv()

            for slot in range(2):
                conv(slot, pair)

        @pl.when(jnp.logical_not(has_prev))
        def _():
            zero = jnp.zeros((CH, COLS), jnp.bfloat16)
            for slot in range(2):
                for k in range(2):
                    hidden[slot, 2 * pair + k] = zero

        for frame in range(2):
            temporal(frame, pair)
        for frame in range(2):
            go_home(frame, pair, step)

    pl.when(jnp.logical_not(skips))(weight_copy(0, q, across, 0).wait_send)
    pl.when(relays)(weight_copy(0, theirs, ring_start, 12).wait_send)
    for j in range(4):
        if j > 0:
            weight_copy(j, q, across, j).wait_send()
        weight_copy(j, q, partner, 4 + j).wait_send()
        weight_copy(j, theirs, partner, 8 + j).wait_send()
    for sends, copy in in_copies:
        pl.when(sends)(copy.wait_send)

    @pl.when(has_next)
    def _():
        for chunk in range(len(CHUNKS)):
            for frame in range(2):
                for sq in range(4):
                    pl.when(jnp.logical_or(chunk < EDGE, edge))(z_copy(chunk, frame, sq).wait_send)

    swap(2, 4, 0).wait_send()

    @pl.when(has_prev)
    def _():
        swap(0, 2, 1).wait_send()

    @pl.loop(0, 3)
    def _(step):
        for frame in range(4):
            each_home(
                frame, pair_of(step), step, lambda far: far.wait_send(), lambda src, dst: None
            )

    pltpu.make_async_copy(back, back, out_recv).wait()


def on_device(latents, space_weight, space_bias, time_weight, time_bias):
    rows_first = latents[:, 0].transpose(1, 0, 2)
    vmem, dma = pltpu.VMEM, pltpu.SemaphoreType.DMA
    bf16, f32 = jnp.bfloat16, jnp.float32
    decoded = pl.pallas_call(
        kernel,
        out_shape=pltpu.VMEM(rows_first.shape, bf16),
        in_specs=[pl.BlockSpec(memory_space=pl.ANY)] * 5,
        out_specs=pl.BlockSpec(memory_space=pl.ANY),
        scratch_shapes=[
            vmem((6, 8, CH, COLS), bf16),
            vmem((6, 6, CH, COLS), bf16),
            vmem((4, 6, CH, COLS), bf16),
            vmem((9, CH, CH), bf16),
            vmem((3, CH, CH), bf16),
            vmem((CH, COLS), f32),
            vmem((SHARD, COLS), f32),
            vmem((2, 1, SHARD), f32),
            dma((6,)),
            dma((len(CHUNKS), 15)),
            dma((len(CHUNKS), 16)),
            dma((len(CHUNKS), 8)),
            dma((len(CHUNKS), 8)),
            dma((2,)),
            dma((2,)),
            dma((13,)),
            dma((12,)),
            dma((3, 4, 4)),
            dma,
        ],
        compiler_params=pltpu.CompilerParams(collective_id=0, has_side_effects=True, vmem_limit_bytes=62 << 20),
        cost_estimate=pl.CostEstimate(flops=6_000_000_000, bytes_accessed=6_000_000, transcendentals=1_200_000),
    )(rows_first, space_weight.transpose(1, 0, 2), time_weight, space_bias[None], time_bias[None])
    return decoded.transpose(1, 0, 2)[:, None]


def solution(mesh):
    return jax.shard_map(
        on_device,
        mesh=mesh,
        in_specs=(
            P("ch", "sp", None, None),
            P("ch", None, None),
            P("ch"),
            P(None, "ch", None),
            P("ch"),
        ),
        out_specs=P("ch", "sp", None, None),
        check_vma=False,
    )
```

time: 54.8 us -> 51.1 us (0.932)
  other arithmetic: 3.1 us -> 0 us
  Pallas kernels: 51.3 us -> 49.9 us
  local copies, waits for them, and re-layouts: 0.01 us -> 1.11 us
    broadcast_in_dim x1 -> x0, other arithmetic: 3.1 us -> none  [on_device(): return total.astype(bf16).transpose(1, 0, 2)[:, None]]
    pallas_call x1, Pallas kernels: 51.3 us -> 49.9 us  [on_device(): pl.pallas_call(kernel, out_shape=pltpu.VMEM(rows_first.shape, bf16), in_s...]
    unnamed x2 -> x1, local copies, waits for them, and re-layouts: 0.01 us -> 1.11 us
where the time goes in v4:
time: 51.1 us
  Pallas kernels  49.9 us (98%)
  local copies, waits for them, and re-layouts  1.11 us (2%)
    pallas_call x1, Pallas kernels, on_device(): pl.pallas_call(kernel, out_shape=pltpu.VMEM(rows_first.shape, bf16), in_s...  49.9 us
    unnamed x1, local copies, waits for them, and re-layouts  1.11 us

profile of v4, /device:TPU:25, one launch (start us, length us, event | category | flops | bytes accessed | tf_op | source)
XLA Modules:
  0.0 51.1 jit_solution(15710196819181353471)
XLA Ops:
  0.0 49.9 %shard_map.55 = bf16[90,64,128]{2,1,0:T(8,128)(2,1)S(1)} custom-call(bf16[90,64,128]{2,1,0:T(8,128)(2,1)} %bitcast.10, bf16[9,64,256]{2,1,0:T(8,128)(2,1)} %bitcast.11, bf16[3,64,256]{2,1,0:T(8,128)(2,1)} %time_hbm.1, f32[1,64]{1,0:T(1,128)} %bitcast.12, f32[1,64]{1,0:T(1,128)} %bitcast.13), custom_call_target="tpu_custom_call" | custom-call | flops 6000000000 | bytes 6000000 | tf_op jit(solution)/shard_map/pallas_call | solution.py:361
  49.9 1.1 %copy.7 = bf16[64,1,90,128]{3,0,2,1:T(8,128)(2,1)} copy(bf16[64,1,90,128]{3,0,2,1:T(8,128)(2,1)S(1)} %bitcast.9) | data formatting | bytes 2949120

commit v5 on v4

--- a/solution.py
+++ b/solution.py
@@ -134,7 +134,7 @@
 
     in_copies = []
     for chunk in range(len(CHUNKS)):
-        if chunk == 1:
+        if chunk == 0:
             for j in range(3):
                 send_weight(j)
         pl.when(jnp.logical_or(chunk < EDGE, edge))(
@@ -290,8 +290,10 @@
             conv(slot, pair)
         for frame in (2, 3):
             temporal(frame, pair)
-        for frame in (2, 3):
-            go_home(frame, pair, step)
+        @pl.when(step < 2)
+        def _():
+            for frame in (2, 3):
+                go_home(frame, pair, step)
 
         for later in (1, 2):
             pl.when(step == later - 1)(functools.partial(arrive, later))
@@ -318,8 +320,15 @@
 
         for frame in range(2):
             temporal(frame, pair)
-        for frame in range(2):
-            go_home(frame, pair, step)
+        @pl.when(step < 2)
+        def _():
+            for frame in range(2):
+                go_home(frame, pair, step)
+
+        @pl.when(step == 2)
+        def _():
+            for ahead in (2, 1, 3, 0):
+                go_home(lax.rem(x + ahead, 4), pair, step)
 
     pl.when(jnp.logical_not(skips))(weight_copy(0, q, across, 0).wait_send)
     pl.when(relays)(weight_copy(0, theirs, ring_start, 12).wait_send)

time: 51.1 us -> 51.2 us (level)
  no operation moved by 1% of the time
where the time goes in v5:
time: 51.2 us; the launch traced here: 51.1 us
  Pallas kernels  49.9 us (97%)
  local copies, waits for them, and re-layouts  1.11 us (2%)
    pallas_call x1, Pallas kernels, on_device(): pl.pallas_call(kernel, out_shape=pltpu.VMEM(rows_first.shape, bf16), in_s...  49.9 us
    unnamed x1, local copies, waits for them, and re-layouts  1.11 us

profile of v5, /device:TPU:25, one launch (start us, length us, event | category | flops | bytes accessed | tf_op | source)
XLA Modules:
  0.0 51.1 jit_solution(11648562973454911066)
XLA Ops:
  0.0 49.9 %shard_map.55 = bf16[90,64,128]{2,1,0:T(8,128)(2,1)S(1)} custom-call(bf16[90,64,128]{2,1,0:T(8,128)(2,1)} %bitcast.10, bf16[9,64,256]{2,1,0:T(8,128)(2,1)} %bitcast.11, bf16[3,64,256]{2,1,0:T(8,128)(2,1)} %time_hbm.1, f32[1,64]{1,0:T(1,128)} %bitcast.12, f32[1,64]{1,0:T(1,128)} %bitcast.13), custom_call_target="tpu_custom_call" | custom-call | flops 6000000000 | bytes 6000000 | tf_op jit(solution)/shard_map/pallas_call | solution.py:370
  50.0 1.1 %copy.7 = bf16[64,1,90,128]{3,0,2,1:T(8,128)(2,1)} copy(bf16[64,1,90,128]{3,0,2,1:T(8,128)(2,1)S(1)} %bitcast.9) | data formatting | bytes 2949120

commit v6 on v5

--- a/solution.py
+++ b/solution.py
@@ -13,7 +13,7 @@
 ORDER = ((1, 2), (3, 0), (2, 3), (0, 2), (1, 0), (3, 2), (2, 0), (0, 3), (1, 3), (3, 1), (2, 2), (1, 1), (3, 3), (2, 1), (0, 1))
 
 
-CHUNKS = ((2, 0, 3, 1), (2, 0, 5, 3), (2, 1, 1, 5), (1, 2, 0, 7))
+CHUNKS = ((4, 0, 3, 1), (2, 1, 1, 5), (1, 2, 0, 7))
 EDGE = len(CHUNKS) - 1
 
 

time: 51.2 us -> 51.3 us (level)
  no operation moved by 1% of the time
where the time goes in v6:
time: 51.3 us; the launch traced here: 51.2 us
  Pallas kernels  50.1 us (98%)
  local copies, waits for them, and re-layouts  1.11 us (2%)
    pallas_call x1, Pallas kernels, on_device(): pl.pallas_call(kernel, out_shape=pltpu.VMEM(rows_first.shape, bf16), in_s...  50.1 us
    unnamed x1, local copies, waits for them, and re-layouts  1.11 us

profile of v6, /device:TPU:25, one launch (start us, length us, event | category | flops | bytes accessed | tf_op | source)
XLA Modules:
  0.0 51.2 jit_solution(17844249393822621952)
XLA Ops:
  0.0 50.1 %shard_map.55 = bf16[90,64,128]{2,1,0:T(8,128)(2,1)S(1)} custom-call(bf16[90,64,128]{2,1,0:T(8,128)(2,1)} %bitcast.10, bf16[9,64,256]{2,1,0:T(8,128)(2,1)} %bitcast.11, bf16[3,64,256]{2,1,0:T(8,128)(2,1)} %time_hbm.1, f32[1,64]{1,0:T(1,128)} %bitcast.12, f32[1,64]{1,0:T(1,128)} %bitcast.13), custom_call_target="tpu_custom_call" | custom-call | flops 6000000000 | bytes 6000000 | tf_op jit(solution)/shard_map/pallas_call | solution.py:370
  50.1 1.1 %copy.7 = bf16[64,1,90,128]{3,0,2,1:T(8,128)(2,1)} copy(bf16[64,1,90,128]{3,0,2,1:T(8,128)(2,1)S(1)} %bitcast.9) | data formatting | bytes 2949120
